TPU v7x, 32 devices: a whole 2x2x4 slice. The times are simulated.
32 devices in a mesh: tiles: 16 (over z, y, x), chan: 2 (over core).
Axes of the slice: x: 2, y: 2, z: 4, core: 2. Of those that a mesh axis runs over, the one named last changes fastest.
Arguments:
- ocean_state: bfloat16 [16, 22, 2, 16, 3072], P('tiles', None, 'chan'), may hold values from -24 to 24
- land_mask: int32 [16, 22], P('tiles'), may hold values from 0 to 1, as said below
- cotangent: bfloat16 [224, 2, 16, 3072], P('tiles', 'chan'), may hold values from -6 to 6
- depth_kernel: float32 [7, 7, 384], P(None, None, 'chan'), may hold values from -1.8 to 1.8
- norm_gain: float32 [384], P('chan'), may hold values from 0.5 to 1.5
- norm_shift: float32 [384], P('chan'), may hold values from -3 to 3
- weight_in: bfloat16 [384, 1536], P(None, 'chan'), may hold values from -0.3125 to 0.3125
- bias_in: float32 [1536], P('chan'), may hold values from -3 to 3
- weight_out: bfloat16 [1536, 384], P('chan'), may hold values from -0.15625 to 0.15625
- bias_out: float32 [384], P('chan'), may hold values from -3 to 3
- layer_scale: float32 [384], P('chan'), may hold values from 0.3 to 1
Outputs:
- block_out: bfloat16 [224, 2, 16, 3072], P('tiles', 'chan')
- grad_state: bfloat16 [16, 22, 2, 16, 3072], P('tiles', None, 'chan')
- grad_kernel: float32 [7, 7, 384], P(None, None, 'chan')
- grad_gain: float32 [384], P('chan')
- grad_shift: float32 [384], P('chan')
- grad_weight_in: float32 [384, 1536], P(None, 'chan')
- grad_bias_in: float32 [1536], P('chan')
- grad_weight_out: float32 [1536, 384], P('chan')
- grad_bias_out: float32 [384], P('chan')
- grad_scale: float32 [384], P('chan')
Inputs may be any that keep to these rules, and one draw needn't show every extreme that they name: `land_mask`: exactly 224 entries are 1, and some band is ocean in all its 22 slots.
All inputs are finite; a program needn't handle non-finite values.
Results may differ from a plain program's by a relative error of at most 0.014.
Values may be sent and summed in bfloat16 or wider, within the bound.
A program may use at most 128 MiB of HBM per device.

v0:
```python
import jax
import jax.numpy as jnp
from jax import lax
from jax.sharding import PartitionSpec as P

EPS = 1e-06
ROOT_TWO_PI = 0.7978845608028654
CUBIC = 0.044715
SWAP = ((0, 1), (1, 0))


def swapped(value):
    return lax.ppermute(value, "chan", SWAP)


def row_halo(field, width):
    count = lax.axis_size("tiles")
    forward = [(i, i + 1) for i in range(count - 1)]
    backward = [(target, source) for source, target in forward]
    low = lax.ppermute(field[field.shape[0] - width :], "tiles", forward)
    high = lax.ppermute(field[:width], "tiles", backward)
    return jnp.concatenate([low, field, high], axis=0)


def gelu_pair(values):
    inner_arg = ROOT_TWO_PI * (values + CUBIC * values * values * values)
    tangent = jnp.tanh(inner_arg)
    gelu_value = 0.5 * values * (1.0 + tangent)
    gelu_slope = 0.5 * (1.0 + tangent) + 0.5 * values * (1.0 - tangent * tangent) * ROOT_TWO_PI * (
        1.0 + 3.0 * CUBIC * values * values
    )
    return (gelu_value, gelu_slope)


def depthwise(padded, kernel):
    span = kernel.shape[0]
    rows, cols = (padded.shape[0] - span + 1, padded.shape[1] - span + 1)
    total = jnp.zeros((rows, cols, padded.shape[2]), jnp.float32)
    for down in range(span):
        for east in range(span):
            window = padded[down : down + rows, east : east + cols]
            total = total + window.astype(jnp.float32) * kernel[down, east]
    return total


def kernel_grads(back, framed, span):
    rows, cols = back.shape[:2]
    back_float = back.astype(jnp.float32)
    sums = []
    for down in range(span):
        for east in range(span):
            window = framed[down : down + rows, east : east + cols].astype(jnp.float32)
            sums.append(jnp.sum(back_float * window, axis=(0, 1)))
    return jnp.stack(sums)


def on_device(
    ocean_state,
    land_mask,
    cotangent,
    depth_kernel,
    norm_gain,
    norm_shift,
    weight_in,
    bias_in,
    weight_out,
    bias_out,
    layer_scale,
):
    devices = lax.axis_size("tiles")
    mine, core = (lax.axis_index("tiles"), lax.axis_index("chan"))
    slots = land_mask.shape[1]
    half = slots // 2
    side = ocean_state.shape[3]
    own = ocean_state.shape[4] // side
    chans = 2 * own
    span = depth_kernel.shape[0]
    margin = span // 2
    listed = cotangent.shape[0]
    width = half * side
    cells = side * width
    group = weight_in.shape[1]
    cap = -(-half // devices)
    masks = lax.all_gather(land_mask[0], "tiles")
    counts = jnp.sum(masks.reshape(2 * devices, half), axis=1)
    ends = jnp.cumsum(counts)
    starts = ends - counts
    home = mine * 2 + core
    my_start = starts[home]
    flags = lax.dynamic_slice(land_mask[0], (core * half,), (half,))
    inclusive = jnp.cumsum(flags)
    lap = jnp.arange(cap, dtype=jnp.int32)
    wanted = (mine - starts)[:, None] % devices + lap * devices
    wanted = jnp.clip((starts[:, None] + wanted) // devices, 0, listed - 1)
    leaving = jnp.take(cotangent[:, 0], wanted.reshape(-1), axis=0)
    landed = lax.all_to_all(leaving, ("tiles", "chan"), 0, 0, tiled=True)
    vectors = jnp.concatenate(
        [depth_kernel.reshape(-1), norm_gain, norm_shift, bias_out, layer_scale, bias_in]
    )
    others = swapped(vectors)

    def both(low, high, lead=()):
        return jnp.concatenate(
            [vectors[low:high].reshape(lead + (-1,)), others[low:high].reshape(lead + (-1,))],
            axis=-1,
        )

    taps = span * span * own
    kernel = both(0, taps, (span, span))
    gain = both(taps, taps + own)
    shift = both(taps + own, taps + 2 * own)
    bias_o = both(taps + 2 * own, taps + 3 * own)
    scale = both(taps + 3 * own, taps + 4 * own)
    bias_h = both(taps + 4 * own, taps + 4 * own + group)
    w_in = jnp.concatenate([weight_in, swapped(weight_in)], axis=1)
    w_in = jnp.where(core == 0, w_in, jnp.concatenate([w_in[own:], w_in[:own]], axis=0))
    w_out = jnp.concatenate([weight_out, swapped(weight_out)], axis=0)
    w_out = jnp.where(core == 0, w_out, jnp.concatenate([w_out[:, own:], w_out[:, :own]], axis=1))
    state = ocean_state[0, :, 0].reshape(slots, side, side, own)
    masked = state * land_mask[0].astype(jnp.bfloat16)[:, None, None, None]
    field = masked.transpose(1, 0, 2, 3).reshape(side, slots * side, own)
    tall = row_halo(field, margin)
    tall = jnp.concatenate([tall[:, slots * side - margin :], tall, tall[:, :margin]], axis=1)
    shape = (tall.shape[0], width + 2 * margin, own)
    kept = lax.dynamic_slice(tall, (0, core * width, 0), shape)
    given = lax.dynamic_slice(tall, (0, (1 - core) * width, 0), shape)
    framed = jnp.concatenate([kept, swapped(given)], axis=2)
    on_land = jnp.repeat(flags, side)[None, :, None] == 0
    mixed = jnp.where(on_land, 0.0, depthwise(framed, kernel)).reshape(cells, chans)
    cell_mean = jnp.sum(mixed, axis=1) / chans
    variance = jnp.sum(mixed * mixed, axis=1) / chans - cell_mean * cell_mean
    factor = lax.rsqrt(variance + EPS)
    normed = (mixed - cell_mean[:, None]) * factor[:, None]
    features = (normed * gain + shift).astype(jnp.bfloat16)
    hidden = jnp.dot(features, w_in, preferred_element_type=jnp.float32) + bias_h
    active, slope = gelu_pair(hidden)
    active = active.astype(jnp.bfloat16)
    branch = jnp.dot(active, w_out, preferred_element_type=jnp.float32) + bias_o
    residual = framed[margin : margin + side, margin : margin + width]
    residual = residual.astype(jnp.float32).reshape(cells, chans)
    block = (residual + scale * branch).astype(jnp.bfloat16)
    block = block.reshape(side, half, side, 2, own).transpose(1, 3, 0, 2, 4)
    block = block.reshape(half * 2, side, side * own)
    target = jnp.arange(devices, dtype=jnp.int32)
    rank = (target - my_start)[:, None] % devices + lap * devices
    source = jnp.sum((inclusive <= rank[..., None]).astype(jnp.int32), axis=-1)
    source = jnp.minimum(source, half - 1)
    part = (jnp.arange(2, dtype=jnp.int32) + core) % 2
    source = source[:, None, :] * 2 + part[None, :, None]
    leaving = jnp.take(block, source.reshape(-1), axis=0)
    finished = lax.all_to_all(leaving, ("tiles", "chan"), 0, 0, tiled=True)
    ranks = jnp.arange(listed, dtype=jnp.int32) * devices + mine
    owner = jnp.sum((ends[None, :] <= ranks[:, None]).astype(jnp.int32), axis=1)
    owner = jnp.minimum(owner, 2 * devices - 1)
    pick = owner * cap + (ranks - starts[owner]) // devices
    block_out = jnp.take(finished, pick, axis=0)[:, None]
    local = jnp.maximum(inclusive - 1, 0)
    pick = ((my_start + local) % devices)[:, None] * 2 + part
    pick = pick * cap + (local // devices)[:, None]
    upstream = jnp.take(landed, pick.reshape(-1), axis=0)
    upstream = upstream.reshape(half, 2, side, side, own).transpose(2, 0, 3, 1, 4)
    upstream = upstream.reshape(side, width, chans).astype(jnp.float32)
    upstream = jnp.where(on_land, 0.0, upstream).reshape(cells, chans)
    scaled = scale * upstream
    scaled_bf = scaled.astype(jnp.bfloat16)
    grad_scale = jnp.sum(upstream * branch, axis=0)
    grad_bias_out = jnp.sum(scaled, axis=0)
    grad_w_out = jnp.dot(active.T, scaled_bf, preferred_element_type=jnp.float32)
    back_hidden = jnp.dot(scaled_bf, w_out.T, preferred_element_type=jnp.float32) * slope
    back_hidden_bf = back_hidden.astype(jnp.bfloat16)
    grad_w_in = jnp.dot(features.T, back_hidden_bf, preferred_element_type=jnp.float32)
    grad_bias_in = jnp.sum(back_hidden, axis=0)
    back_features = jnp.dot(back_hidden_bf, w_in.T, preferred_element_type=jnp.float32)
    grad_w_in = jnp.where(
        core == 0, grad_w_in, jnp.concatenate([grad_w_in[own:], grad_w_in[:own]], axis=0)
    )
    grad_w_out = jnp.where(
        core == 0, grad_w_out, jnp.concatenate([grad_w_out[:, own:], grad_w_out[:, :own]], axis=1)
    )
    norm_cells = float(devices * listed * side * side) ** 0.5
    grad_w_in = (grad_w_in[:, :group] + swapped(grad_w_in[:, group:])) / norm_cells
    grad_w_out = (grad_w_out[:group] + swapped(grad_w_out[group:])) / norm_cells
    grad_w_in, grad_w_out = lax.psum((grad_w_in, grad_w_out), "tiles")
    back_normed = back_features * gain
    grad_gain = jnp.sum(back_features * normed, axis=0)
    grad_shift = jnp.sum(back_features, axis=0)
    first = jnp.sum(back_normed, axis=1) / chans
    second = jnp.sum(back_normed * normed, axis=1) / chans
    back_mixed = factor[:, None] * (back_normed - first[:, None] - normed * second[:, None])
    back = back_mixed.astype(jnp.bfloat16).reshape(side, width, chans)
    back_tall = row_halo(back, margin)
    rims = swapped(jnp.concatenate([back_tall[:, :margin], back_tall[:, width - margin :]], axis=1))
    rims = jnp.concatenate([rims[..., own:], rims[..., :own]], axis=2)
    back_framed = jnp.concatenate([rims[:, margin:], back_tall, rims[:, :margin]], axis=1)
    grad_field = depthwise(back_framed, kernel[::-1, ::-1])
    grad_field = jnp.where(on_land, 0.0, grad_field).astype(jnp.bfloat16)
    grad_kept, grad_got = (grad_field[..., :own], swapped(grad_field[..., own:]))
    grad_cells = jnp.where(
        core == 0,
        jnp.concatenate([grad_kept, grad_got], axis=1),
        jnp.concatenate([grad_got, grad_kept], axis=1),
    )
    grad_cells = grad_cells.reshape(side, slots, side, own).transpose(1, 0, 2, 3)
    grad_state = grad_cells.reshape(1, slots, 1, side, side * own)
    grad_kernel = kernel_grads(back, framed, span)
    by_channel = jnp.concatenate(
        [grad_kernel, jnp.stack([grad_gain, grad_shift, grad_bias_out, grad_scale])], axis=0
    )
    keep = jnp.concatenate([by_channel[:, :own].reshape(-1), grad_bias_in[:group]])
    give = jnp.concatenate([by_channel[:, own:].reshape(-1), grad_bias_in[group:]])
    summed = lax.psum(keep + swapped(give), "tiles") / norm_cells
    ends_at = span * span * own
    rows = summed[ends_at : ends_at + 4 * own].reshape(4, own)
    return (
        block_out,
        grad_state,
        summed[:ends_at].reshape(span, span, own),
        rows[0],
        rows[1],
        grad_w_in,
        summed[ends_at + 4 * own :],
        grad_w_out,
        rows[2],
        rows[3],
    )


def solution(mesh):
    in_specs = (
        P("tiles", None, "chan", None, None),
        P("tiles", None),
        P("tiles", "chan", None, None),
        P(None, None, "chan"),
        P("chan"),
        P("chan"),
        P(None, "chan"),
        P("chan"),
        P("chan", None),
        P("chan"),
        P("chan"),
    )
    out_specs = (
        P("tiles", "chan", None, None),
        P("tiles", None, "chan", None, None),
        P(None, None, "chan"),
        P("chan"),
        P("chan"),
        P(None, "chan"),
        P("chan"),
        P("chan", None),
        P("chan"),
        P("chan"),
    )
    return jax.shard_map(
        on_device, mesh=mesh, in_specs=in_specs, out_specs=out_specs, check_vma=False
    )
```

profile of v0, /device:TPU:0, one launch (start us, length us, event | category | flops | bytes accessed | tf_op | source)
XLA Modules:
  0.0 676.1 jit_solution(16829266664952852585)
XLA Ops:
  7.2 1.0 reshape.695
  9.5 2.2 copy.101
  12.8 6.0 reshape_squeeze.3
  18.8 2.1 fusion.257
  21.3 1.3 collective-permute-start.1
  22.6 1.0 copy.96
  23.6 5.8 collective-permute-start
  29.7 49.5 %all-gather = s32[16,1,22]{2,1,0:T(1,128)S(1)} all-gather(s32[1,1,22]{2,1,0:T(1,128)S(1)} %bitcast.111), channel_id=1, replica_groups=mesh['tiles'=16,'chan'=2] {'tiles'}, dimensions={0}, use_global_device_ids=true | all-gather | bytes 1496 | tf_op jit(solution)/shard_map/all_gather | solution.py:84
  83.2 2.4 gather_fusion.3
  85.6 3.9 broadcast_select_fusion.1
  89.5 4.1 all-to-all-start.1
  98.2 2.1 copy_multiply_fusion
  100.3 1.2 copy.99
  101.6 2.0 copy.98
  103.6 15.4 %fusion.137 = bf16[22,358,192]{2,1,0:T(8,128)(2,1)S(1)} fusion(bf16[3,352,192]{2,1,0:T(8,128)(2,1)S(1)} %copy.99, bf16[16,352,192]{2,1,0:T(8,128)(2,1)S(1)} %bitcast.98, bf16[3,352,192]{2,1,0:T(8,128)(2,1)} %copy.98), kind=kLoop, calls=%fused_computation.354 | loop fusion | flops 27219456 | bytes 5998080 | tf_op jit(solution)/shard_map/concatenate | solution.py:123
  119.1 3.9 constant_dynamic-slice_fusion
  130.1 1.1 constant_dynamic-update-slice_fusion
  131.2 2.7 fusion.197
  134.0 1.1 fusion.244
  135.1 99.4 %fusion.237 = (f32[16,176]{1,0:T(8,128)S(1)}, f32[16,176]{1,0:T(8,128)S(1)}, f32[16,176,384]{2,1,0:T(8,128)}) fusion(f32[384]{0:T(512)S(1)} %get-tuple-element.173, bf16[22,182,192]{2,1,0:T(8,128)(2,1)} %collective-permute-done.2, bf16[22,182,192]{2,1,0:T(8,128)(2,1)S(1)} %get-tuple-element.186, f32[384]{0:T(512)} %get-tuple-element.126, ...), kind=kLoop, calls=%fused_computation.619 | loop fusion | flops 321153536 | bytes 7498416 | tf_op jit(solution)/shard_map/reduce_sum | solution.py:130
  235.0 4.8 fusion.146
  239.9 1.6 add_convert_fusion
  241.5 1.4 copy-done.7
  242.9 12.8 %multiply_convert_fusion = (bf16[2816,1536]{1,0:T(8,128)(2,1)}, f32[2816,1536]{1,0:T(8,128)}) fusion(f32[1536]{0:T(1024)S(1)} %pad_maximum_fusion.10, bf16[2816,384]{1,0:T(8,128)(2,1)S(1)} %add_convert_fusion, bf16[384,1536]{1,0:T(8,128)(2,1)S(1)} %constant_dynamic-update-slice_fusion, bf16[192,1536]{1,0:T(8,128)(2,1)S(1)} %copy-done.24, ...), kind=kOutput, calls=%fused_computation.63 | convolution fusion | flops 3368091648 | bytes 30480384 | tf_op jit(solution)/shard_map/dot_general | solution.py:135
  255.7 4.0 gather_fusion.4
  259.7 5.0 gather.32
  264.7 5.9 convert_bitcast_fusion
  270.6 7.9 %reshape.705 = f32[2816,384]{1,0:T(8,128)} reshape(f32[16,11,16,2,192]{4,3,2,1,0:T(2,128)} %convert_bitcast_fusion) | data formatting | bytes 8650752 | tf_op jit(solution)/shard_map/convert_element_type | solution.py:162
  278.5 19.4 %fusion.250 = (f32[1536]{0:T(1024)S(1)}, bf16[2816,1536]{1,0:T(8,128)(2,1)S(1)}) fusion(f32[2816,1536]{1,0:T(8,128)} %get-tuple-element.220, f32[1536]{0:T(1024)S(1)} %pad_maximum_fusion.10, bf16[768,384]{0,1:T(8,128)(2,1)} %collective-permute-done.5, bf16[768,384]{0,1:T(8,128)(2,1)} %copy.101, bf16[1536,192]{0,1:T(8,128)(2,1)} %get-tuple-element.200, ...), kind=kOutput, calls=%fused_computation.631 | convolution fusion | flops 3421272576 | bytes 32653568 | tf_op jit(solution)/shard_map/dot_general | solution.py:169
  297.9 5.0 fusion.132
  302.9 7.9 %multiply_reduce_fusion.1 = (f32[384]{0:T(512)S(1)}, f32[2816]{0:T(1024)S(1)}, f32[2816]{0:T(1024)S(1)}, f32[384]{0:T(512)S(1)}, f32[2816,384]{1,0:T(8,128)}) fusion(f32[16,176,384]{2,1,0:T(8,128)S(1)} %bitcast.95, f32[2816]{0:T(1024)S(1)} %add_rsqrt_fusion, f32[2816]{0:T(1024)S(1)} %div.87, f32[384]{0:T(512)S(1)} %get-tuple-element.228, ...), kind=kOutput, calls=%fused_computation.340 | convolution fusion | flops 3334563328 | bytes 19710464 | tf_op jit(solution)/shard_map/dot_general | solution.py:173
  310.9 6.3 fusion.7
  317.3 9.9 %fusion.236 = f32[1536,384]{0,1:T(8,128)} fusion(bf16[2816,1536]{1,0:T(8,128)(2,1)} %get-tuple-element.219, f32[2816,384]{1,0:T(8,128)} %reshape.705, f32[384]{0:T(512)S(1)} %get-tuple-element.226, pred[2816]{0:T(1024)(128)(4,1)S(1)} %copy-done.69), kind=kOutput, calls=%fused_computation.618 | convolution fusion | flops 3325132800 | bytes 15339776 | tf_op jit(solution)/shard_map/dot_general | solution.py:168
  327.2 9.8 %multiply_reduce_fusion = (f32[384]{0:T(512)S(1)}, bf16[2816,384]{1,0:T(8,128)(2,1)}) fusion(f32[2816,384]{1,0:T(8,128)S(1)} %bitcast.105, pred[2816]{0:T(1024)(128)(4,1)S(1)} %copy-done.69, f32[384]{0:T(512)S(1)} %get-tuple-element.226, f32[16,176,384]{2,1,0:T(8,128)} %fusion.146, f32[384]{0:T(512)S(1)} %copy-done.71, ...), kind=kOutput, calls=%fused_computation.339 | convolution fusion | flops 3334766080 | bytes 21830912 | tf_op jit(solution)/shard_map/dot_general | solution.py:138
  337.8 2.2 multiply_convert_fusion.1
  340.9 7.7 %fusion.85 = (f32[384]{0:T(512)S(1)}, f32[384]{0:T(512)S(1)}, f32[384]{0:T(512)S(1)}, f32[384]{0:T(512)S(1)}) fusion(bf16[16,176,384]{2,1,0:T(8,128)(2,1)S(1)} %bitcast.85, bf16[22,182,192]{2,1,0:T(8,128)(2,1)} %collective-permute-done.2, bf16[22,182,192]{2,1,0:T(8,128)(2,1)S(1)} %copy-done.4), kind=kLoop, calls=%fused_computation.290 | loop fusion | flops 27032064 | bytes 5243904 | tf_op jit(solution)/shard_map/reduce_sum | solution.py:53
  348.7 17.9 %fusion.125 = (f32[384]{0:T(512)S(1)}, f32[384]{0:T(512)S(1)}, f32[384]{0:T(512)S(1)}, f32[384]{0:T(512)S(1)}, f32[384]{0:T(512)S(1)}, /*index=5*/f32[384]{0:T(5...) fusion(bf16[16,176,384]{2,1,0:T(8,128)(2,1)S(1)} %bitcast.86, bf16[22,182,192]{2,1,0:T(8,128)(2,1)} %collective-permute-done.2, ...), kind=kLoop, calls=%fused_computation.330 | loop fusion | flops 59470464 | bytes 5251584 | tf_op jit(solution)/shard_map/reduce_sum | solution.py:53
  366.8 17.0 %fusion.126 = (f32[384]{0:T(512)S(1)}, f32[384]{0:T(512)S(1)}, f32[384]{0:T(512)S(1)}, f32[384]{0:T(512)S(1)}, f32[384]{0:T(512)S(1)}, /*index=5*/f32[384]{0:T(5...) fusion(bf16[16,176,384]{2,1,0:T(8,128)(2,1)S(1)} %bitcast.87, bf16[22,182,192]{2,1,0:T(8,128)(2,1)} %collective-permute-done.2, ...), kind=kLoop, calls=%fused_computation.331 | loop fusion | flops 59470464 | bytes 5251584 | tf_op jit(solution)/shard_map/reduce_sum | solution.py:53
  383.9 17.8 %fusion.129 = (f32[384]{0:T(512)S(1)}, f32[384]{0:T(512)S(1)}, f32[384]{0:T(512)S(1)}, f32[384]{0:T(512)S(1)}, f32[384]{0:T(512)S(1)}, /*index=5*/f32[384]{0:T(5...) fusion(bf16[16,176,384]{2,1,0:T(8,128)(2,1)S(1)} %bitcast.88, bf16[22,182,192]{2,1,0:T(8,128)(2,1)} %collective-permute-done.2, ...), kind=kLoop, calls=%fused_computation.334 | loop fusion | flops 59470464 | bytes 5251584 | tf_op jit(solution)/shard_map/reduce_sum | solution.py:53
  401.8 17.4 %fusion.128 = (f32[384]{0:T(512)S(1)}, f32[384]{0:T(512)S(1)}, f32[384]{0:T(512)S(1)}, f32[384]{0:T(512)S(1)}, f32[384]{0:T(512)S(1)}, /*index=5*/f32[384]{0:T(5...) fusion(bf16[16,176,384]{2,1,0:T(8,128)(2,1)S(1)} %bitcast.89, bf16[22,182,192]{2,1,0:T(8,128)(2,1)} %collective-permute-done.2, ...), kind=kLoop, calls=%fused_computation.333 | loop fusion | flops 59470464 | bytes 5251584 | tf_op jit(solution)/shard_map/reduce_sum | solution.py:53
  419.2 17.3 %fusion.127 = (f32[384]{0:T(512)S(1)}, f32[384]{0:T(512)S(1)}, f32[384]{0:T(512)S(1)}, f32[384]{0:T(512)S(1)}, f32[384]{0:T(512)S(1)}, /*index=5*/f32[384]{0:T(5...) fusion(bf16[16,176,384]{2,1,0:T(8,128)(2,1)S(1)} %bitcast.90, bf16[22,182,192]{2,1,0:T(8,128)(2,1)} %collective-permute-done.2, ...), kind=kLoop, calls=%fused_computation.332 | loop fusion | flops 59470464 | bytes 5251584 | tf_op jit(solution)/shard_map/reduce_sum | solution.py:53
  438.1 1.3 collective-permute-start.7
  439.4 4.7 collective-permute-start.6
  444.2 1.8 fusion.241
  446.4 1.1 slice.1161
  448.9 1.2 slice.1166
  450.8 7.5 %reshape.698 = bf16[16,11,16,2,192]{4,3,2,1,0:T(2,128)(2,1)} reshape(bf16[2816,384]{1,0:T(8,128)(2,1)} %get-tuple-element.184) | data formatting | bytes 4325376 | tf_op jit(solution)/shard_map/reshape | solution.py:142
  458.3 4.0 copy.123
  462.3 5.8 reshape.699
  468.0 4.2 gather_fusion.1
  472.9 4.0 broadcast_select_fusion.2
  476.9 6.8 %all-to-all-start = ((bf16[32,16,3072]{2,1,0:T(8,128)(2,1)}), bf16[32,16,3072]{2,1,0:T(8,128)(2,1)}, u32[]{:S(2)}, u32[]{:S(2)}) async-start(bf16[32,16,3072]{2,1,0:T(8,128)(2,1)} %broadcast_select_fusion.2), calls=%async_computation | async-start | bytes 6291456 | tf_op jit(solution)/shard_map/all_to_all | solution.py:151
  484.0 6.3 maximum_maximum_fusion
  490.3 2.5 fusion.196
  492.8 2.5 fusion.195
  495.3 58.0 %select_convert_fusion = bf16[16,176,384]{2,1,0:T(8,128)(2,1)S(1)} fusion(bf16[16,176,384]{2,1,0:T(8,128)(2,1)} %bitcast.93, bf16[3,176,384]{2,1,0:T(8,128)(2,1)S(1)} %collective-permute-done.7, bf16[3,176,384]{2,1,0:T(8,128)(2,1)} %copy-done.14, bf16[22,179,384]{2,1,0:T(8,128)(2,1)} %get-tuple-element.188, ...), kind=kLoop, calls=%fused_computation.341 | loop fusion | flops 166526976 | bytes 96044720 | tf_op jit(solution)/shard_map/convert_element_type | solution.py:196
  553.3 1.8 fusion.242
  556.1 77.4 %psum.21 = f32[10944]{0:T(1024)S(1)} all-reduce(f32[10944]{0:T(1024)S(1)} %maximum_add_fusion), channel_id=1, replica_groups=mesh['tiles'=16,'chan'=2] {'tiles'}, use_global_device_ids=true, to_apply=%region_63.64 | all-reduce | flops 10944 | bytes 87552 | tf_op jit(solution)/shard_map/psum | solution.py:211
  636.8 4.0 reshape.701
  640.8 19.2 %all-reduce.3.cloned.1.call-done = (f32[384,768]{1,0:T(8,128)}, f32[768,384]{0,1:T(8,128)}) async-done(((f32[384,768]{1,0:T(8,128)}, f32[768,384]{0,1:T(8,128)}), (f32[384,768]{1,0:T(8,128)}, f32[768,384]{0,1:T(8,128)})) %all-reduce.3.cloned.1.call-update) | async-done | bytes 2359312 | tf_op jit(solution)/shard_map/psum | solution.py:183
  660.0 2.8 copy.111
  662.8 2.6 gather_fusion.2
  665.4 1.3 fusion.193
  666.7 2.4 copy.127
  (341 shorter events, 29.7 us)
Async XLA Ops:
  7.2 76.0 %copy-start = (bf16[14,1,16,3072]{3,2,1,0:T(8,128)(2,1)S(1)}, bf16[14,1,16,3072]{3,2,1,0:T(8,128)(2,1)}, u32[]{:S(2)}) copy-start(bf16[14,1,16,3072]{3,2,1,0:T(8,128)(2,1)} %param.13) | copy-start | bytes 4128772
  9.0 116.6 %collective-permute-start.3 = (f32[10944]{0:T(1024)S(1)}, f32[10944]{0:T(1024)S(1)}, u32[]{:S(2)}, u32[]{:S(2)}) collective-permute-start(f32[10944]{0:T(1024)S(1)} %concatenate.132), channel_id=1, source_target_pairs={{0,1},{1,0},{2,3},{3,2},{4,5},{5,4},{6,7},{7,6},{8,9},{9,8},{10,11... | collective-permute-start | bytes 131336 | tf_op jit(solution)/shard_map/ppermute | solution.py:13
  11.7 119.6 %collective-permute-start.5 = (bf16[768,384]{0,1:T(8,128)(2,1)}, bf16[768,384]{0,1:T(8,128)(2,1)}, u32[]{:S(2)}, u32[]{:S(2)}) collective-permute-start(bf16[768,384]{0,1:T(8,128)(2,1)} %copy.101), channel_id=1, source_target_pairs={{0,1},{1,0},{2,3},{3,2},{4,5},{5,4},{6,7},{7,6},{8,9},{9,8},{10,11... | collective-permute-start | bytes 1769480 | tf_op jit(solution)/shard_map/ppermute | solution.py:13
  11.7 118.4 %collective-permute-start.4 = (bf16[384,768]{1,0:T(8,128)(2,1)}, bf16[384,768]{1,0:T(8,128)(2,1)}, u32[]{:S(2)}, u32[]{:S(2)}) collective-permute-start(bf16[384,768]{1,0:T(8,128)(2,1)} %param.17), channel_id=1, source_target_pairs={{0,1},{1,0},{2,3},{3,2},{4,5},{5,4},{6,7},{7,6},{8,9},{9,8},{10,11... | collective-permute-start | bytes 1769480 | tf_op jit(solution)/shard_map/ppermute | solution.py:13
  21.3 79.0 %collective-permute-start.1 = (bf16[3,352,192]{1,2,0:T(8,128)(2,1)S(1)}, bf16[3,352,192]{1,2,0:T(8,128)(2,1)}, u32[]{:S(2)}, u32[]{:S(2)}) collective-permute-start(bf16[3,352,192]{1,2,0:T(8,128)(2,1)S(1)} %copy.97), channel_id=1, source_target_pairs={{2,0},{4,2},{6,4},{8,6},{10,8},{12,10},{14,12},{16,14},{18,16},{20... | collective-permute-start | bytes 1216520 | tf_op jit(solution)/shard_map/ppermute | solution.py:21
  23.6 78.0 %collective-permute-start = (bf16[3,352,192]{1,2,0:T(8,128)(2,1)}, bf16[3,352,192]{1,2,0:T(8,128)(2,1)}, u32[]{:S(2)}, u32[]{:S(2)}) collective-permute-start(bf16[3,352,192]{1,2,0:T(8,128)(2,1)} %copy.96), channel_id=1, source_target_pairs={{0,2},{2,4},{4,6},{6,8},{8,10},{10,12},{12,14},{14,16},{16,18},{18... | collective-permute-start | bytes 1216520 | tf_op jit(solution)/shard_map/ppermute | solution.py:20
  89.5 166.2 %all-to-all-start.1 = ((bf16[32,16,3072]{2,1,0:T(8,128)(2,1)}), bf16[32,16,3072]{2,1,0:T(8,128)(2,1)}, u32[]{:S(2)}, u32[]{:S(2)}) async-start(bf16[32,16,3072]{2,1,0:T(8,128)(2,1)} %broadcast_select_fusion.1), calls=%async_computation.1 | async-start | bytes 6291456 | tf_op jit(solution)/shard_map/all_to_all | solution.py:96
  123.0 112.0 %copy-start.3 = (bf16[22,182,192]{2,1,0:T(8,128)(2,1)}, bf16[22,182,192]{2,1,0:T(8,128)(2,1)S(1)}, u32[]{:S(2)}) copy-start(bf16[22,182,192]{2,1,0:T(8,128)(2,1)S(1)} %get-tuple-element.186) | copy-start | bytes 4612612
  123.0 12.1 %collective-permute-start.2 = (bf16[22,182,192]{2,1,0:T(8,128)(2,1)}, bf16[22,182,192]{2,1,0:T(8,128)(2,1)}, u32[]{:S(2)}, u32[]{:S(2)}) collective-permute-start(bf16[22,182,192]{2,1,0:T(8,128)(2,1)} %get-tuple-element.185), channel_id=1, source_target_pairs={{0,1},{1,0},{2,3},{3,2},{4,5},{5,4},{6,7},{7,6},{8,9},{9,8},{10,11... | collective-permute-start | bytes 4612616 | tf_op jit(solution)/shard_map/ppermute | solution.py:13
  127.2 107.2 %copy-start.26 = (f32[384]{0:T(512)}, f32[384]{0:T(512)S(1)}, u32[]{:S(2)}) copy-start(f32[384]{0:T(512)S(1)} %get-tuple-element.170) | copy-start | bytes 4612
  127.3 107.2 %copy-start.27 = (f32[384]{0:T(512)}, f32[384]{0:T(512)S(1)}, u32[]{:S(2)}) copy-start(f32[384]{0:T(512)S(1)} %get-tuple-element.171) | copy-start | bytes 4612
  127.3 107.2 %copy-start.28 = (f32[384]{0:T(512)}, f32[384]{0:T(512)S(1)}, u32[]{:S(2)}) copy-start(f32[384]{0:T(512)S(1)} %get-tuple-element.172) | copy-start | bytes 4612
  127.3 107.2 %copy-start.29 = (f32[384]{0:T(512)}, f32[384]{0:T(512)S(1)}, u32[]{:S(2)}) copy-start(f32[384]{0:T(512)S(1)} %get-tuple-element.173) | copy-start | bytes 4612
  127.4 107.1 %copy-start.30 = (f32[384]{0:T(512)}, f32[384]{0:T(512)S(1)}, u32[]{:S(2)}) copy-start(f32[384]{0:T(512)S(1)} %get-tuple-element.161) | copy-start | bytes 4612
  127.4 107.1 %copy-start.31 = (f32[384]{0:T(512)}, f32[384]{0:T(512)S(1)}, u32[]{:S(2)}) copy-start(f32[384]{0:T(512)S(1)} %get-tuple-element.162) | copy-start | bytes 4612
  127.4 107.1 %copy-start.32 = (f32[384]{0:T(512)}, f32[384]{0:T(512)S(1)}, u32[]{:S(2)}) copy-start(f32[384]{0:T(512)S(1)} %get-tuple-element.163) | copy-start | bytes 4612
  127.4 107.1 %copy-start.33 = (f32[384]{0:T(512)}, f32[384]{0:T(512)S(1)}, u32[]{:S(2)}) copy-start(f32[384]{0:T(512)S(1)} %get-tuple-element.164) | copy-start | bytes 4612
  127.4 107.1 %copy-start.34 = (f32[384]{0:T(512)}, f32[384]{0:T(512)S(1)}, u32[]{:S(2)}) copy-start(f32[384]{0:T(512)S(1)} %get-tuple-element.165) | copy-start | bytes 4612
  127.4 107.1 %copy-start.35 = (f32[384]{0:T(512)}, f32[384]{0:T(512)S(1)}, u32[]{:S(2)}) copy-start(f32[384]{0:T(512)S(1)} %get-tuple-element.166) | copy-start | bytes 4612
  127.5 107.1 %copy-start.36 = (f32[384]{0:T(512)}, f32[384]{0:T(512)S(1)}, u32[]{:S(2)}) copy-start(f32[384]{0:T(512)S(1)} %get-tuple-element.167) | copy-start | bytes 4612
  127.5 107.1 %copy-start.37 = (f32[384]{0:T(512)}, f32[384]{0:T(512)S(1)}, u32[]{:S(2)}) copy-start(f32[384]{0:T(512)S(1)} %get-tuple-element.168) | copy-start | bytes 4612
  127.5 107.1 %copy-start.38 = (f32[384]{0:T(512)}, f32[384]{0:T(512)S(1)}, u32[]{:S(2)}) copy-start(f32[384]{0:T(512)S(1)} %get-tuple-element.169) | copy-start | bytes 4612
  127.6 107.0 %copy-start.39 = (f32[384]{0:T(512)}, f32[384]{0:T(512)S(1)}, u32[]{:S(2)}) copy-start(f32[384]{0:T(512)S(1)} %get-tuple-element.152) | copy-start | bytes 4612
  127.6 107.0 %copy-start.40 = (f32[384]{0:T(512)}, f32[384]{0:T(512)S(1)}, u32[]{:S(2)}) copy-start(f32[384]{0:T(512)S(1)} %get-tuple-element.153) | copy-start | bytes 4612
  127.6 107.0 %copy-start.41 = (f32[384]{0:T(512)}, f32[384]{0:T(512)S(1)}, u32[]{:S(2)}) copy-start(f32[384]{0:T(512)S(1)} %get-tuple-element.154) | copy-start | bytes 4612
  127.6 107.0 %copy-start.42 = (f32[384]{0:T(512)}, f32[384]{0:T(512)S(1)}, u32[]{:S(2)}) copy-start(f32[384]{0:T(512)S(1)} %get-tuple-element.155) | copy-start | bytes 4612
  127.6 107.0 %copy-start.43 = (f32[384]{0:T(512)}, f32[384]{0:T(512)S(1)}, u32[]{:S(2)}) copy-start(f32[384]{0:T(512)S(1)} %get-tuple-element.156) | copy-start | bytes 4612
  127.6 107.0 %copy-start.44 = (f32[384]{0:T(512)}, f32[384]{0:T(512)S(1)}, u32[]{:S(2)}) copy-start(f32[384]{0:T(512)S(1)} %get-tuple-element.157) | copy-start | bytes 4612
  127.7 107.0 %copy-start.45 = (f32[384]{0:T(512)}, f32[384]{0:T(512)S(1)}, u32[]{:S(2)}) copy-start(f32[384]{0:T(512)S(1)} %get-tuple-element.158) | copy-start | bytes 4612
  127.7 107.0 %copy-start.46 = (f32[384]{0:T(512)}, f32[384]{0:T(512)S(1)}, u32[]{:S(2)}) copy-start(f32[384]{0:T(512)S(1)} %get-tuple-element.159) | copy-start | bytes 4612
  127.7 107.0 %copy-start.47 = (f32[384]{0:T(512)}, f32[384]{0:T(512)S(1)}, u32[]{:S(2)}) copy-start(f32[384]{0:T(512)S(1)} %get-tuple-element.160) | copy-start | bytes 4612
  127.8 106.8 %copy-start.48 = (f32[384]{0:T(512)}, f32[384]{0:T(512)S(1)}, u32[]{:S(2)}) copy-start(f32[384]{0:T(512)S(1)} %get-tuple-element.143) | copy-start | bytes 4612
  127.8 106.8 %copy-start.49 = (f32[384]{0:T(512)}, f32[384]{0:T(512)S(1)}, u32[]{:S(2)}) copy-start(f32[384]{0:T(512)S(1)} %get-tuple-element.144) | copy-start | bytes 4612
  127.8 106.8 %copy-start.50 = (f32[384]{0:T(512)}, f32[384]{0:T(512)S(1)}, u32[]{:S(2)}) copy-start(f32[384]{0:T(512)S(1)} %get-tuple-element.145) | copy-start | bytes 4612
  127.8 106.8 %copy-start.51 = (f32[384]{0:T(512)}, f32[384]{0:T(512)S(1)}, u32[]{:S(2)}) copy-start(f32[384]{0:T(512)S(1)} %get-tuple-element.146) | copy-start | bytes 4612
  127.8 106.8 %copy-start.52 = (f32[384]{0:T(512)}, f32[384]{0:T(512)S(1)}, u32[]{:S(2)}) copy-start(f32[384]{0:T(512)S(1)} %get-tuple-element.147) | copy-start | bytes 4612
  127.8 106.8 %copy-start.53 = (f32[384]{0:T(512)}, f32[384]{0:T(512)S(1)}, u32[]{:S(2)}) copy-start(f32[384]{0:T(512)S(1)} %get-tuple-element.148) | copy-start | bytes 4612
  127.9 106.8 %copy-start.54 = (f32[384]{0:T(512)}, f32[384]{0:T(512)S(1)}, u32[]{:S(2)}) copy-start(f32[384]{0:T(512)S(1)} %get-tuple-element.149) | copy-start | bytes 4612
  127.9 106.8 %copy-start.55 = (f32[384]{0:T(512)}, f32[384]{0:T(512)S(1)}, u32[]{:S(2)}) copy-start(f32[384]{0:T(512)S(1)} %get-tuple-element.150) | copy-start | bytes 4612
  127.9 106.8 %copy-start.56 = (f32[384]{0:T(512)}, f32[384]{0:T(512)S(1)}, u32[]{:S(2)}) copy-start(f32[384]{0:T(512)S(1)} %get-tuple-element.151) | copy-start | bytes 4612
  128.6 106.1 %copy-start.57 = (f32[384]{0:T(512)}, f32[384]{0:T(512)S(1)}, u32[]{:S(2)}) copy-start(f32[384]{0:T(512)S(1)} %get-tuple-element.134) | copy-start | bytes 4612
  128.6 106.2 %copy-start.58 = (f32[384]{0:T(512)}, f32[384]{0:T(512)S(1)}, u32[]{:S(2)}) copy-start(f32[384]{0:T(512)S(1)} %get-tuple-element.135) | copy-start | bytes 4612
  128.6 106.2 %copy-start.59 = (f32[384]{0:T(512)}, f32[384]{0:T(512)S(1)}, u32[]{:S(2)}) copy-start(f32[384]{0:T(512)S(1)} %get-tuple-element.136) | copy-start | bytes 4612
  128.6 106.2 %copy-start.60 = (f32[384]{0:T(512)}, f32[384]{0:T(512)S(1)}, u32[]{:S(2)}) copy-start(f32[384]{0:T(512)S(1)} %get-tuple-element.137) | copy-start | bytes 4612
  128.6 106.2 %copy-start.61 = (f32[384]{0:T(512)}, f32[384]{0:T(512)S(1)}, u32[]{:S(2)}) copy-start(f32[384]{0:T(512)S(1)} %get-tuple-element.138) | copy-start | bytes 4612
  128.6 106.2 %copy-start.62 = (f32[384]{0:T(512)}, f32[384]{0:T(512)S(1)}, u32[]{:S(2)}) copy-start(f32[384]{0:T(512)S(1)} %get-tuple-element.139) | copy-start | bytes 4612
  131.2 110.3 %copy-start.17 = (bf16[384,1536]{1,0:T(8,128)(2,1)}, bf16[384,1536]{1,0:T(8,128)(2,1)S(1)}, u32[]{:S(2)}) copy-start(bf16[384,1536]{1,0:T(8,128)(2,1)S(1)} %constant_dynamic-update-slice_fusion) | copy-start | bytes 3538948
  270.6 32.3 %slice-start = ((s8[4325376]{0:T(1024)(128)(4,1)}), s8[131072]{0:T(1024)(128)(4,1)S(1)}, s32[]{:S(2)}) async-start(s8[4325376]{0:T(1024)(128)(4,1)} %bitcast.94), calls=%async_computation.3 | async-start | bytes 262144
  278.5 19.4 %copy-start.8 = (bf16[2816,384]{1,0:T(8,128)(2,1)S(1)}, bf16[2816,384]{1,0:T(8,128)(2,1)}, u32[]{:S(2)}) copy-start(bf16[2816,384]{1,0:T(8,128)(2,1)} %copy-done.7) | copy-start | bytes 6488068
  278.5 24.4 %slice-start.1 = ((s8[4325376]{0:T(1024)(128)(4,1)}), s8[4194304]{0:T(1024)(128)(4,1)S(1)}, s32[]{:S(2)}) async-start(s8[4325376]{0:T(1024)(128)(4,1)} %bitcast.94), calls=%async_computation.4 | async-start | bytes 8388608
  310.9 16.3 %slice-start.6 = ((s8[4325376]{0:T(1024)(128)(4,1)}), s8[131072]{0:T(1024)(128)(4,1)S(1)}, s32[]{:S(2)}) async-start(s8[4325376]{0:T(1024)(128)(4,1)} %bitcast.104), calls=%async_computation.9 | async-start | bytes 262144
  317.3 20.4 %slice-start.2 = ((s8[4325376]{0:T(1024)(128)(4,1)}), s8[4194304]{0:T(1024)(128)(4,1)S(1)}, s32[]{:S(2)}) async-start(s8[4325376]{0:T(1024)(128)(4,1)} %bitcast.96), calls=%async_computation.5 | async-start | bytes 8388608
  317.3 20.4 %slice-start.4 = ((s8[4325376]{0:T(1024)(128)(4,1)}), s8[4194304]{0:T(1024)(128)(4,1)S(1)}, s32[]{:S(2)}) async-start(s8[4325376]{0:T(1024)(128)(4,1)} %bitcast.102), calls=%async_computation.7 | async-start | bytes 8388608
  340.0 132.2 %copy-start.2 = (bf16[2816,384]{1,0:T(8,128)(2,1)}, bf16[2816,384]{1,0:T(8,128)(2,1)S(1)}, u32[]{:S(2)}) copy-start(bf16[2816,384]{1,0:T(8,128)(2,1)S(1)} %multiply_convert_fusion.1) | copy-start | bytes 6488068
  437.9 117.4 %collective-permute-start.10 = (f32[10944]{0:T(1024)}, f32[10944]{0:T(1024)}, u32[]{:S(2)}, u32[]{:S(2)}) collective-permute-start(f32[10944]{0:T(1024)} %pad_maximum_fusion.9), channel_id=1, source_target_pairs={{0,1},{1,0},{2,3},{3,2},{4,5},{5,4},{6,7},{7,6},{8,9},{9,8},{10,11... | collective-permute-start | bytes 131336 | tf_op jit(solution)/shard_map/ppermute | solution.py:13
  438.1 34.1 %collective-permute-start.7 = (bf16[3,176,384]{2,1,0:T(8,128)(2,1)}, bf16[3,176,384]{2,1,0:T(8,128)(2,1)S(1)}, u32[]{:S(2)}, u32[]{:S(2)}) collective-permute-start(bf16[3,176,384]{2,1,0:T(8,128)(2,1)} %bitcast.109), channel_id=1, source_target_pairs={{2,0},{4,2},{6,4},{8,6},{10,8},{12,10},{14,12},{16,14},{18,16},{20... | collective-permute-start | bytes 1216520 | tf_op jit(solution)/shard_map/ppermute | solution.py:21
  439.4 32.8 %collective-permute-start.6 = (bf16[3,176,384]{2,1,0:T(8,128)(2,1)S(1)}, bf16[3,176,384]{2,1,0:T(8,128)(2,1)S(1)}, u32[]{:S(2)}, u32[]{:S(2)}) collective-permute-start(bf16[3,176,384]{2,1,0:T(8,128)(2,1)S(1)} %bitcast.108), channel_id=1, source_target_pairs={{0,2},{2,4},{4,6},{6,8},{8,10},{10,12},{12,14},{14,16},{16,18},{18... | collective-permute-start | bytes 1216520 | tf_op jit(solution)/shard_map/ppermute | solution.py:20
  447.5 42.8 %collective-permute-start.11 = (f32[384,768]{1,0:T(8,128)}, f32[384,768]{1,0:T(8,128)}, u32[]{:S(2)}, u32[]{:S(2)}) collective-permute-start(f32[384,768]{1,0:T(8,128)} %slice.1161), channel_id=1, source_target_pairs={{0,1},{1,0},{2,3},{3,2},{4,5},{5,4},{6,7},{7,6},{8,9},{9,8},{10,11... | collective-permute-start | bytes 3538952 | tf_op jit(solution)/shard_map/ppermute | solution.py:13
  450.8 42.0 %collective-permute-start.12 = (f32[768,384]{0,1:T(8,128)}, f32[768,384]{0,1:T(8,128)}, u32[]{:S(2)}, u32[]{:S(2)}) collective-permute-start(f32[768,384]{0,1:T(8,128)} %slice.1166), channel_id=1, source_target_pairs={{0,1},{1,0},{2,3},{3,2},{4,5},{5,4},{6,7},{7,6},{8,9},{9,8},{10,11... | collective-permute-start | bytes 3538952 | tf_op jit(solution)/shard_map/ppermute | solution.py:13
  472.3 11.4 %collective-permute-start.8 = (bf16[22,6,384]{2,1,0:T(8,128)(2,1)S(1)}, bf16[22,6,384]{2,1,0:T(8,128)(2,1)S(1)}, u32[]{:S(2)}, u32[]{:S(2)}) collective-permute-start(bf16[22,6,384]{2,1,0:T(8,128)(2,1)S(1)} %fusion.207), channel_id=1, source_target_pairs={{0,1},{1,0},{2,3},{3,2},{4,5},{5,4},{6,7},{7,6},{8,9},{9,8},{10,11... | collective-permute-start | bytes 304136 | tf_op jit(solution)/shard_map/ppermute | solution.py:13
  476.9 185.9 %all-to-all-start = ((bf16[32,16,3072]{2,1,0:T(8,128)(2,1)}), bf16[32,16,3072]{2,1,0:T(8,128)(2,1)}, u32[]{:S(2)}, u32[]{:S(2)}) async-start(bf16[32,16,3072]{2,1,0:T(8,128)(2,1)} %broadcast_select_fusion.2), calls=%async_computation | async-start | bytes 6291456 | tf_op jit(solution)/shard_map/all_to_all | solution.py:151
  483.7 176.3 %all-reduce.3.cloned.1.call-start = ((), (), s32[]{:S(2)}) async-start(), calls=%async_computation.2 | async-start | bytes 4718592 | tf_op jit(solution)/shard_map/psum | solution.py:183
  555.1 80.5 %collective-permute-start.9 = (bf16[16,176,192]{2,1,0:T(8,128)(2,1)}, bf16[16,176,192]{2,1,0:T(8,128)(2,1)S(1)}, u32[]{:S(2)}, u32[]{:S(2)}) collective-permute-start(bf16[16,176,192]{2,1,0:T(8,128)(2,1)} %get-tuple-element.196), channel_id=1, source_target_pairs={{0,1},{1,0},{2,3},{3,2},{4,5},{5,4},{6,7},{7,6},{8,9},{9,8},{10,11... | collective-permute-start | bytes 3244040 | tf_op jit(solution)/shard_map/ppermute | solution.py:13
  636.8 28.6 %copy-start.70 = (pred[14]{0:T(512)(128)(4,1)S(1)}, pred[14]{0:T(512)(128)(4,1)}, u32[]{:S(2)}) copy-start(pred[14]{0:T(512)(128)(4,1)} %compare_and_fusion.3) | copy-start | bytes 46
  (36 other events, 242.7 us)
Sparse Core Ops, SparseCore 0:
  495.4 164.5 all-reduce.2
where the time goes:
time: 682 us; the launch traced here: 676 us
  other arithmetic  329 us (48%)
  blocking collectives  127 us (19%)
  local copies, waits for them, and re-layouts  93.9 us (14%)
  matrix products  64.9 us (10%)
  starting transfers between devices  26.3 us (4%)
  waiting for transfers between devices  19.2 us (3%)
  between operations  16 us (2%)
    reduce_sum x1, other arithmetic, on_device(): cell_mean = jnp.sum(mixed, axis=1) / chans  99.4 us
    reduce_sum x6, other arithmetic, kernel_grads(): sums.append(jnp.sum(back_float * window, axis=(0, 1)))  95.2 us
    psum x1, blocking collectives, on_device(): summed = lax.psum(keep + swapped(give), 'tiles') / norm_cells  77.4 us
    convert_element_type x1, other arithmetic, on_device(): grad_field = jnp.where(on_land, 0.0, grad_field).astype(jnp.bfloat16)  58 us
    all_gather x1, blocking collectives, on_device(): masks = lax.all_gather(land_mask[0], 'tiles')  49.5 us
    dot_general x1, matrix products, on_device(): jnp.dot(scaled_bf, w_out.T, preferred_element_type=jnp.float32) * slope  19.4 us
    psum x1, waiting for transfers between devices, on_device(): grad_w_in, grad_w_out = lax.psum((grad_w_in, grad_w_out), 'tiles')  19.2 us
    concatenate x1, other arithmetic, on_device(): jnp.concatenate([tall[:, slots * side - margin:], tall, tall[:, :margin]]...  15.4 us
  transfers between devices with their start and end apart: 16, of which 1 were waited for; matrix products, arithmetic and copies ran while one was open for 44% of the time, Pallas kernels for 0%

commit v1 on v0

--- a/solution.py
+++ b/solution.py
@@ -208,7 +208,7 @@
     )
     keep = jnp.concatenate([by_channel[:, :own].reshape(-1), grad_bias_in[:group]])
     give = jnp.concatenate([by_channel[:, own:].reshape(-1), grad_bias_in[group:]])
-    summed = lax.psum(keep + swapped(give), "tiles") / norm_cells
+    summed = jnp.sum(lax.all_gather(keep + swapped(give), "tiles"), axis=0) / norm_cells
     ends_at = span * span * own
     rows = summed[ends_at : ends_at + 4 * own].reshape(4, own)
     return (

time: 682 us -> 707 us (1.037)
  waiting for transfers between devices: 19.2 us -> 118 us
  blocking collectives: 127 us -> 49.5 us
    unnamed x1 -> x2, waiting for transfers between devices: 0.02 us -> 115 us
    psum x1 -> x0, blocking collectives: 77.4 us -> none  [on_device(): summed = lax.psum(keep + swapped(give), 'tiles') / norm_cells]
    psum x1 -> x0, waiting for transfers between devices: 19.2 us -> none  [on_device(): grad_w_in, grad_w_out = lax.psum((grad_w_in, grad_w_out), 'tiles')]
  transfers between devices with their start and end apart: 16 -> 16, of which waited for: 1 -> 3; matrix products, arithmetic and copies ran while one was open for 44% -> 42% of each run, Pallas kernels for 0% -> 0%
where the time goes in v1:
time: 707 us; the launch traced here: 701 us
  other arithmetic  329 us (47%)
  waiting for transfers between devices  118 us (17%)
  local copies, waits for them, and re-layouts  95.9 us (14%)
  matrix products  65.5 us (9%)
  blocking collectives  49.5 us (7%)
  starting transfers between devices  26.4 us (4%)
  between operations  16.9 us (2%)
    unnamed x2, waiting for transfers between devices  115 us
    reduce_sum x1, other arithmetic, on_device(): cell_mean = jnp.sum(mixed, axis=1) / chans  100 us
    reduce_sum x6, other arithmetic, kernel_grads(): sums.append(jnp.sum(back_float * window, axis=(0, 1)))  95.2 us
    convert_element_type x1, other arithmetic, on_device(): grad_field = jnp.where(on_land, 0.0, grad_field).astype(jnp.bfloat16)  57.5 us
    all_gather x1, blocking collectives, on_device(): masks = lax.all_gather(land_mask[0], 'tiles')  49.5 us
    dot_general x1, matrix products, on_device(): jnp.dot(scaled_bf, w_out.T, preferred_element_type=jnp.float32) * slope  19.4 us
    concatenate x1, other arithmetic, on_device(): jnp.concatenate([tall[:, slots * side - margin:], tall, tall[:, :margin]]...  15.4 us
  transfers between devices with their start and end apart: 16, of which 3 were waited for; matrix products, arithmetic and copies ran while one was open for 42% of the time, Pallas kernels for 0%

profile of v1, /device:TPU:0, one launch (start us, length us, event | category | flops | bytes accessed | tf_op | source)
XLA Modules:
  0.0 700.8 jit_solution(7046174342536918175)
XLA Ops:
  9.5 2.2 copy.101
  12.8 6.0 reshape_squeeze.3
  18.8 2.1 fusion.258
  21.3 1.3 collective-permute-start.1
  23.6 5.8 collective-permute-start
  29.7 49.5 %all-gather.1 = s32[16,1,22]{2,1,0:T(1,128)S(1)} all-gather(s32[1,1,22]{2,1,0:T(1,128)S(1)} %bitcast.112), channel_id=1, replica_groups=mesh['tiles'=16,'chan'=2] {'tiles'}, dimensions={0}, use_global_device_ids=true | all-gather | bytes 1496 | tf_op jit(solution)/shard_map/all_gather | solution.py:84
  83.2 2.4 gather_fusion.3
  85.6 3.9 broadcast_select_fusion.1
  89.5 4.1 all-to-all-start.1
  96.7 2.1 copy_multiply_fusion
  98.8 1.2 copy.99
  100.1 2.0 copy.98
  102.1 15.4 %fusion.137 = bf16[22,358,192]{2,1,0:T(8,128)(2,1)S(1)} fusion(bf16[3,352,192]{2,1,0:T(8,128)(2,1)S(1)} %copy.99, bf16[16,352,192]{2,1,0:T(8,128)(2,1)S(1)} %bitcast.99, bf16[3,352,192]{2,1,0:T(8,128)(2,1)} %copy.98), kind=kLoop, calls=%fused_computation.354 | loop fusion | flops 27219456 | bytes 5998080 | tf_op jit(solution)/shard_map/concatenate | solution.py:123
  117.6 3.9 constant_dynamic-slice_fusion
  129.8 1.3 pad_maximum_fusion.10
  131.1 1.1 constant_dynamic-update-slice_fusion
  132.3 2.7 fusion.197
  135.0 1.1 fusion.245
  136.1 100.4 %fusion.238 = (f32[16,176]{1,0:T(8,128)S(1)}, f32[16,176]{1,0:T(8,128)S(1)}, f32[16,176,384]{2,1,0:T(8,128)}) fusion(f32[384]{0:T(512)S(1)} %get-tuple-element.173, bf16[22,182,192]{2,1,0:T(8,128)(2,1)} %collective-permute-done.2, bf16[22,182,192]{2,1,0:T(8,128)(2,1)S(1)} %get-tuple-element.187, f32[384]{0:T(512)S(1)} %get-tuple-element.126, ...), kind=kLoop, calls=%fused_computation.620 | loop fusion | flops 321153536 | bytes 7498416 | tf_op jit(solution)/shard_map/reduce_sum | solution.py:130
  237.1 4.8 fusion.146
  241.9 1.6 add_convert_fusion
  243.6 1.4 copy-done.9
  244.9 13.5 %multiply_convert_fusion = (bf16[2816,1536]{1,0:T(8,128)(2,1)}, f32[2816,1536]{1,0:T(8,128)}) fusion(f32[1536]{0:T(1024)} %pad_maximum_fusion.10, bf16[2816,384]{1,0:T(8,128)(2,1)S(1)} %add_convert_fusion, bf16[384,1536]{1,0:T(8,128)(2,1)S(1)} %constant_dynamic-update-slice_fusion, bf16[192,1536]{1,0:T(8,128)(2,1)S(1)} %copy-done.27, ...), kind=kOutput, calls=%fused_computation.63 | convolution fusion | flops 3368091648 | bytes 30480384 | tf_op jit(solution)/shard_map/dot_general | solution.py:135
  258.4 4.1 gather_fusion.4
  262.6 5.0 gather.32
  267.6 5.9 convert_bitcast_fusion
  273.5 7.9 %reshape.705 = f32[2816,384]{1,0:T(8,128)} reshape(f32[16,11,16,2,192]{4,3,2,1,0:T(2,128)} %convert_bitcast_fusion) | data formatting | bytes 8650752 | tf_op jit(solution)/shard_map/convert_element_type | solution.py:162
  281.4 19.4 %fusion.251 = (f32[1536]{0:T(1024)S(1)}, bf16[2816,1536]{1,0:T(8,128)(2,1)S(1)}) fusion(f32[2816,1536]{1,0:T(8,128)} %get-tuple-element.221, f32[1536]{0:T(1024)} %pad_maximum_fusion.10, bf16[768,384]{0,1:T(8,128)(2,1)} %collective-permute-done.5, bf16[768,384]{0,1:T(8,128)(2,1)} %copy.101, bf16[1536,192]{0,1:T(8,128)(2,1)} %get-tuple-element.201, ...), kind=kOutput, calls=%fused_computation.632 | convolution fusion | flops 3421272576 | bytes 32653568 | tf_op jit(solution)/shard_map/dot_general | solution.py:169
  300.8 5.0 fusion.132
  305.9 7.9 %multiply_reduce_fusion.1 = (f32[384]{0:T(512)S(1)}, f32[2816]{0:T(1024)S(1)}, f32[2816]{0:T(1024)S(1)}, f32[384]{0:T(512)S(1)}, f32[2816,384]{1,0:T(8,128)}) fusion(f32[16,176,384]{2,1,0:T(8,128)S(1)} %bitcast.96, f32[2816]{0:T(1024)S(1)} %add_rsqrt_fusion, f32[2816]{0:T(1024)S(1)} %div.87, f32[384]{0:T(512)S(1)} %copy-done.69, ...), kind=kOutput, calls=%fused_computation.340 | convolution fusion | flops 3334563328 | bytes 19710464 | tf_op jit(solution)/shard_map/dot_general | solution.py:173
  313.8 6.3 fusion.7
  320.2 9.9 %fusion.237 = f32[1536,384]{0,1:T(8,128)} fusion(bf16[2816,1536]{1,0:T(8,128)(2,1)} %get-tuple-element.220, f32[2816,384]{1,0:T(8,128)} %reshape.705, f32[384]{0:T(512)S(1)} %copy-done.72, pred[2816]{0:T(1024)(128)(4,1)S(1)} %copy-done.78), kind=kOutput, calls=%fused_computation.619 | convolution fusion | flops 3325132800 | bytes 15339776 | tf_op jit(solution)/shard_map/dot_general | solution.py:168
  330.2 9.8 %multiply_reduce_fusion = (f32[384]{0:T(512)S(1)}, bf16[2816,384]{1,0:T(8,128)(2,1)}) fusion(f32[2816,384]{1,0:T(8,128)S(1)} %bitcast.106, pred[2816]{0:T(1024)(128)(4,1)S(1)} %copy-done.78, f32[384]{0:T(512)S(1)} %copy-done.72, f32[16,176,384]{2,1,0:T(8,128)} %fusion.146, f32[384]{0:T(512)S(1)} %copy-done.81, bf16[2816,1536]{1,0:T(8,128)(2,1)} %get-tuple-element.220, ...), kind=kOutput, calls=%fused_computation.339 | convolution fusion | flops 3334766080 | bytes 21830912 | tf_op jit(solution)/shard_map/dot_general | solution.py:138
  340.1 2.2 multiply_convert_fusion.1
  343.2 7.7 %fusion.85 = (f32[384]{0:T(512)S(1)}, f32[384]{0:T(512)S(1)}, f32[384]{0:T(512)S(1)}, f32[384]{0:T(512)S(1)}) fusion(bf16[16,176,384]{2,1,0:T(8,128)(2,1)S(1)} %bitcast.86, bf16[22,182,192]{2,1,0:T(8,128)(2,1)} %collective-permute-done.2, bf16[22,182,192]{2,1,0:T(8,128)(2,1)S(1)} %copy-done.6), kind=kLoop, calls=%fused_computation.290 | loop fusion | flops 27032064 | bytes 5243904 | tf_op jit(solution)/shard_map/reduce_sum | solution.py:53
  351.0 17.9 %fusion.125 = (f32[384]{0:T(512)S(1)}, f32[384]{0:T(512)S(1)}, f32[384]{0:T(512)S(1)}, f32[384]{0:T(512)S(1)}, f32[384]{0:T(512)S(1)}, /*index=5*/f32[384]{0:T(5...) fusion(bf16[16,176,384]{2,1,0:T(8,128)(2,1)S(1)} %bitcast.87, bf16[22,182,192]{2,1,0:T(8,128)(2,1)} %collective-permute-done.2, ...), kind=kLoop, calls=%fused_computation.330 | loop fusion | flops 59470464 | bytes 5251584 | tf_op jit(solution)/shard_map/reduce_sum | solution.py:53
  369.1 17.0 %fusion.126 = (f32[384]{0:T(512)S(1)}, f32[384]{0:T(512)S(1)}, f32[384]{0:T(512)S(1)}, f32[384]{0:T(512)S(1)}, f32[384]{0:T(512)S(1)}, /*index=5*/f32[384]{0:T(5...) fusion(bf16[16,176,384]{2,1,0:T(8,128)(2,1)S(1)} %bitcast.88, bf16[22,182,192]{2,1,0:T(8,128)(2,1)} %collective-permute-done.2, ...), kind=kLoop, calls=%fused_computation.331 | loop fusion | flops 59470464 | bytes 5251584 | tf_op jit(solution)/shard_map/reduce_sum | solution.py:53
  386.2 17.8 %fusion.129 = (f32[384]{0:T(512)S(1)}, f32[384]{0:T(512)S(1)}, f32[384]{0:T(512)S(1)}, f32[384]{0:T(512)S(1)}, f32[384]{0:T(512)S(1)}, /*index=5*/f32[384]{0:T(5...) fusion(bf16[16,176,384]{2,1,0:T(8,128)(2,1)S(1)} %bitcast.89, bf16[22,182,192]{2,1,0:T(8,128)(2,1)} %collective-permute-done.2, ...), kind=kLoop, calls=%fused_computation.334 | loop fusion | flops 59470464 | bytes 5251584 | tf_op jit(solution)/shard_map/reduce_sum | solution.py:53
  404.1 17.4 %fusion.128 = (f32[384]{0:T(512)S(1)}, f32[384]{0:T(512)S(1)}, f32[384]{0:T(512)S(1)}, f32[384]{0:T(512)S(1)}, f32[384]{0:T(512)S(1)}, /*index=5*/f32[384]{0:T(5...) fusion(bf16[16,176,384]{2,1,0:T(8,128)(2,1)S(1)} %bitcast.90, bf16[22,182,192]{2,1,0:T(8,128)(2,1)} %collective-permute-done.2, ...), kind=kLoop, calls=%fused_computation.333 | loop fusion | flops 59470464 | bytes 5251584 | tf_op jit(solution)/shard_map/reduce_sum | solution.py:53
  421.5 17.3 %fusion.127 = (f32[384]{0:T(512)S(1)}, f32[384]{0:T(512)S(1)}, f32[384]{0:T(512)S(1)}, f32[384]{0:T(512)S(1)}, f32[384]{0:T(512)S(1)}, /*index=5*/f32[384]{0:T(5...) fusion(bf16[16,176,384]{2,1,0:T(8,128)(2,1)S(1)} %bitcast.91, bf16[22,182,192]{2,1,0:T(8,128)(2,1)} %collective-permute-done.2, ...), kind=kLoop, calls=%fused_computation.332 | loop fusion | flops 59470464 | bytes 5251584 | tf_op jit(solution)/shard_map/reduce_sum | solution.py:53
  440.0 1.4 collective-permute-start.7
  441.4 4.7 collective-permute-start.6
  446.1 1.8 fusion.242
  448.3 1.1 slice.1161
  450.9 1.2 slice.1166
  452.8 7.5 %reshape.698 = bf16[16,11,16,2,192]{4,3,2,1,0:T(2,128)(2,1)} reshape(bf16[2816,384]{1,0:T(8,128)(2,1)} %get-tuple-element.185) | data formatting | bytes 4325376 | tf_op jit(solution)/shard_map/reshape | solution.py:142
  460.3 4.0 copy.123
  464.3 5.8 reshape.699
  470.0 4.2 gather_fusion.1
  474.2 4.0 broadcast_select_fusion.2
  478.2 6.9 all-to-all-start
  487.0 6.3 maximum_maximum_fusion
  493.3 2.5 fusion.196
  495.7 2.5 fusion.195
  498.2 57.5 %select_convert_fusion = bf16[16,176,384]{2,1,0:T(8,128)(2,1)S(1)} fusion(bf16[16,176,384]{2,1,0:T(8,128)(2,1)} %bitcast.94, bf16[3,176,384]{2,1,0:T(8,128)(2,1)S(1)} %collective-permute-done.7, bf16[3,176,384]{2,1,0:T(8,128)(2,1)} %copy-done.16, bf16[22,179,384]{2,1,0:T(8,128)(2,1)} %get-tuple-element.189, ...), kind=kLoop, calls=%fused_computation.341 | loop fusion | flops 166526976 | bytes 96044720 | tf_op jit(solution)/shard_map/convert_element_type | solution.py:196
  555.8 1.8 fusion.243
  558.7 2.2 collective-permute-done.9
  562.3 4.0 reshape.701
  566.4 115.0 %all-reduce.4.cloned.1.call-done = (f32[175104]{0:T(1024)}, f32[384,768]{1,0:T(8,128)}, f32[768,384]{0,1:T(8,128)}) async-done(((f32[175104]{0:T(1024)}, f32[384,768]{1,0:T(8,128)}, f32[768,384]{0,1:T(8,128)}), (f32[175104]{0:T(1024)}, f32[384,768]{1,0:T(8,128)}, f32[768,384]{0,1:T(8,128)})) %all-reduce.4.cloned.1.call-update) | async-done | bytes 3059728
  681.3 1.3 reshape.746
  684.2 2.8 copy.111
  687.6 2.5 gather_fusion.2
  690.1 1.3 fusion.193
  691.4 2.4 copy.129
  (364 shorter events, 31.0 us)
Async XLA Ops:
  7.2 76.0 %copy-start = (bf16[14,1,16,3072]{3,2,1,0:T(8,128)(2,1)S(1)}, bf16[14,1,16,3072]{3,2,1,0:T(8,128)(2,1)}, u32[]{:S(2)}) copy-start(bf16[14,1,16,3072]{3,2,1,0:T(8,128)(2,1)} %param.13) | copy-start | bytes 4128772
  9.0 116.2 %collective-permute-start.3 = (f32[10944]{0:T(1024)S(1)}, f32[10944]{0:T(1024)S(1)}, u32[]{:S(2)}, u32[]{:S(2)}) collective-permute-start(f32[10944]{0:T(1024)S(1)} %concatenate.132), channel_id=1, source_target_pairs={{0,1},{1,0},{2,3},{3,2},{4,5},{5,4},{6,7},{7,6},{8,9},{9,8},{10,11... | collective-permute-start | bytes 131336 | tf_op jit(solution)/shard_map/ppermute | solution.py:13
  11.7 120.6 %collective-permute-start.5 = (bf16[768,384]{0,1:T(8,128)(2,1)}, bf16[768,384]{0,1:T(8,128)(2,1)}, u32[]{:S(2)}, u32[]{:S(2)}) collective-permute-start(bf16[768,384]{0,1:T(8,128)(2,1)} %copy.101), channel_id=1, source_target_pairs={{0,1},{1,0},{2,3},{3,2},{4,5},{5,4},{6,7},{7,6},{8,9},{9,8},{10,11... | collective-permute-start | bytes 1769480 | tf_op jit(solution)/shard_map/ppermute | solution.py:13
  11.7 119.4 %collective-permute-start.4 = (bf16[384,768]{1,0:T(8,128)(2,1)}, bf16[384,768]{1,0:T(8,128)(2,1)}, u32[]{:S(2)}, u32[]{:S(2)}) collective-permute-start(bf16[384,768]{1,0:T(8,128)(2,1)} %param.17), channel_id=1, source_target_pairs={{0,1},{1,0},{2,3},{3,2},{4,5},{5,4},{6,7},{7,6},{8,9},{9,8},{10,11... | collective-permute-start | bytes 1769480 | tf_op jit(solution)/shard_map/ppermute | solution.py:13
  21.3 77.6 %collective-permute-start.1 = (bf16[3,352,192]{1,2,0:T(8,128)(2,1)S(1)}, bf16[3,352,192]{1,2,0:T(8,128)(2,1)}, u32[]{:S(2)}, u32[]{:S(2)}) collective-permute-start(bf16[3,352,192]{1,2,0:T(8,128)(2,1)S(1)} %copy.97), channel_id=1, source_target_pairs={{2,0},{4,2},{6,4},{8,6},{10,8},{12,10},{14,12},{16,14},{18,16},{20... | collective-permute-start | bytes 1216520 | tf_op jit(solution)/shard_map/ppermute | solution.py:21
  23.6 76.5 %collective-permute-start = (bf16[3,352,192]{1,2,0:T(8,128)(2,1)}, bf16[3,352,192]{1,2,0:T(8,128)(2,1)}, u32[]{:S(2)}, u32[]{:S(2)}) collective-permute-start(bf16[3,352,192]{1,2,0:T(8,128)(2,1)} %copy.96), channel_id=1, source_target_pairs={{0,2},{2,4},{4,6},{6,8},{8,10},{10,12},{12,14},{14,16},{16,18},{18... | collective-permute-start | bytes 1216520 | tf_op jit(solution)/shard_map/ppermute | solution.py:20
  89.5 168.9 %all-to-all-start.1 = ((bf16[32,16,3072]{2,1,0:T(8,128)(2,1)}), bf16[32,16,3072]{2,1,0:T(8,128)(2,1)}, u32[]{:S(2)}, u32[]{:S(2)}) async-start(bf16[32,16,3072]{2,1,0:T(8,128)(2,1)} %broadcast_select_fusion.1), calls=%async_computation.1 | async-start | bytes 6291456 | tf_op jit(solution)/shard_map/all_to_all | solution.py:96
  117.6 13.5 %copy-start.19 = (bf16[384,1536]{1,0:T(8,128)(2,1)S(1)}, bf16[384,1536]{1,0:T(8,128)(2,1)}, u32[]{:S(2)}) copy-start(bf16[384,1536]{1,0:T(8,128)(2,1)} %constant_dynamic-update-slice_fusion.1) | copy-start | bytes 3538948
  121.5 115.6 %copy-start.5 = (bf16[22,182,192]{2,1,0:T(8,128)(2,1)}, bf16[22,182,192]{2,1,0:T(8,128)(2,1)S(1)}, u32[]{:S(2)}) copy-start(bf16[22,182,192]{2,1,0:T(8,128)(2,1)S(1)} %get-tuple-element.187) | copy-start | bytes 4612612
  121.5 14.6 %collective-permute-start.2 = (bf16[22,182,192]{2,1,0:T(8,128)(2,1)}, bf16[22,182,192]{2,1,0:T(8,128)(2,1)}, u32[]{:S(2)}, u32[]{:S(2)}) collective-permute-start(bf16[22,182,192]{2,1,0:T(8,128)(2,1)} %get-tuple-element.186), channel_id=1, source_target_pairs={{0,1},{1,0},{2,3},{3,2},{4,5},{5,4},{6,7},{7,6},{8,9},{9,8},{10,11... | collective-permute-start | bytes 4612616 | tf_op jit(solution)/shard_map/ppermute | solution.py:13
  127.6 108.9 %copy-start.29 = (f32[384]{0:T(512)}, f32[384]{0:T(512)S(1)}, u32[]{:S(2)}) copy-start(f32[384]{0:T(512)S(1)} %get-tuple-element.167) | copy-start | bytes 4612
  127.6 108.9 %copy-start.30 = (f32[384]{0:T(512)}, f32[384]{0:T(512)S(1)}, u32[]{:S(2)}) copy-start(f32[384]{0:T(512)S(1)} %get-tuple-element.168) | copy-start | bytes 4612
  127.6 108.9 %copy-start.31 = (f32[384]{0:T(512)}, f32[384]{0:T(512)S(1)}, u32[]{:S(2)}) copy-start(f32[384]{0:T(512)S(1)} %get-tuple-element.169) | copy-start | bytes 4612
  127.8 108.7 %copy-start.32 = (f32[384]{0:T(512)}, f32[384]{0:T(512)S(1)}, u32[]{:S(2)}) copy-start(f32[384]{0:T(512)S(1)} %get-tuple-element.152) | copy-start | bytes 4612
  127.8 108.7 %copy-start.33 = (f32[384]{0:T(512)}, f32[384]{0:T(512)S(1)}, u32[]{:S(2)}) copy-start(f32[384]{0:T(512)S(1)} %get-tuple-element.153) | copy-start | bytes 4612
  127.8 108.7 %copy-start.34 = (f32[384]{0:T(512)}, f32[384]{0:T(512)S(1)}, u32[]{:S(2)}) copy-start(f32[384]{0:T(512)S(1)} %get-tuple-element.154) | copy-start | bytes 4612
  127.8 108.7 %copy-start.35 = (f32[384]{0:T(512)}, f32[384]{0:T(512)S(1)}, u32[]{:S(2)}) copy-start(f32[384]{0:T(512)S(1)} %get-tuple-element.155) | copy-start | bytes 4612
  127.8 108.7 %copy-start.36 = (f32[384]{0:T(512)}, f32[384]{0:T(512)S(1)}, u32[]{:S(2)}) copy-start(f32[384]{0:T(512)S(1)} %get-tuple-element.156) | copy-start | bytes 4612
  127.8 108.7 %copy-start.37 = (f32[384]{0:T(512)}, f32[384]{0:T(512)S(1)}, u32[]{:S(2)}) copy-start(f32[384]{0:T(512)S(1)} %get-tuple-element.157) | copy-start | bytes 4612
  127.8 108.7 %copy-start.38 = (f32[384]{0:T(512)}, f32[384]{0:T(512)S(1)}, u32[]{:S(2)}) copy-start(f32[384]{0:T(512)S(1)} %get-tuple-element.158) | copy-start | bytes 4612
  127.8 108.7 %copy-start.39 = (f32[384]{0:T(512)}, f32[384]{0:T(512)S(1)}, u32[]{:S(2)}) copy-start(f32[384]{0:T(512)S(1)} %get-tuple-element.159) | copy-start | bytes 4612
  127.8 108.7 %copy-start.40 = (f32[384]{0:T(512)}, f32[384]{0:T(512)S(1)}, u32[]{:S(2)}) copy-start(f32[384]{0:T(512)S(1)} %get-tuple-element.160) | copy-start | bytes 4612
  128.0 108.6 %copy-start.41 = (f32[384]{0:T(512)}, f32[384]{0:T(512)S(1)}, u32[]{:S(2)}) copy-start(f32[384]{0:T(512)S(1)} %get-tuple-element.143) | copy-start | bytes 4612
  128.0 108.6 %copy-start.42 = (f32[384]{0:T(512)}, f32[384]{0:T(512)S(1)}, u32[]{:S(2)}) copy-start(f32[384]{0:T(512)S(1)} %get-tuple-element.144) | copy-start | bytes 4612
  128.0 108.6 %copy-start.43 = (f32[384]{0:T(512)}, f32[384]{0:T(512)S(1)}, u32[]{:S(2)}) copy-start(f32[384]{0:T(512)S(1)} %get-tuple-element.145) | copy-start | bytes 4612
  128.0 108.6 %copy-start.44 = (f32[384]{0:T(512)}, f32[384]{0:T(512)S(1)}, u32[]{:S(2)}) copy-start(f32[384]{0:T(512)S(1)} %get-tuple-element.146) | copy-start | bytes 4612
  128.0 108.6 %copy-start.45 = (f32[384]{0:T(512)}, f32[384]{0:T(512)S(1)}, u32[]{:S(2)}) copy-start(f32[384]{0:T(512)S(1)} %get-tuple-element.147) | copy-start | bytes 4612
  128.0 108.6 %copy-start.46 = (f32[384]{0:T(512)}, f32[384]{0:T(512)S(1)}, u32[]{:S(2)}) copy-start(f32[384]{0:T(512)S(1)} %get-tuple-element.148) | copy-start | bytes 4612
  128.0 108.6 %copy-start.47 = (f32[384]{0:T(512)}, f32[384]{0:T(512)S(1)}, u32[]{:S(2)}) copy-start(f32[384]{0:T(512)S(1)} %get-tuple-element.149) | copy-start | bytes 4612
  128.0 108.6 %copy-start.48 = (f32[384]{0:T(512)}, f32[384]{0:T(512)S(1)}, u32[]{:S(2)}) copy-start(f32[384]{0:T(512)S(1)} %get-tuple-element.150) | copy-start | bytes 4612
  128.0 108.6 %copy-start.49 = (f32[384]{0:T(512)}, f32[384]{0:T(512)S(1)}, u32[]{:S(2)}) copy-start(f32[384]{0:T(512)S(1)} %get-tuple-element.151) | copy-start | bytes 4612
  128.2 108.5 %copy-start.50 = (f32[384]{0:T(512)}, f32[384]{0:T(512)S(1)}, u32[]{:S(2)}) copy-start(f32[384]{0:T(512)S(1)} %get-tuple-element.134) | copy-start | bytes 4612
  128.2 108.5 %copy-start.51 = (f32[384]{0:T(512)}, f32[384]{0:T(512)S(1)}, u32[]{:S(2)}) copy-start(f32[384]{0:T(512)S(1)} %get-tuple-element.135) | copy-start | bytes 4612
  128.2 108.5 %copy-start.52 = (f32[384]{0:T(512)}, f32[384]{0:T(512)S(1)}, u32[]{:S(2)}) copy-start(f32[384]{0:T(512)S(1)} %get-tuple-element.136) | copy-start | bytes 4612
  128.2 108.5 %copy-start.53 = (f32[384]{0:T(512)}, f32[384]{0:T(512)S(1)}, u32[]{:S(2)}) copy-start(f32[384]{0:T(512)S(1)} %get-tuple-element.137) | copy-start | bytes 4612
  128.2 108.5 %copy-start.54 = (f32[384]{0:T(512)}, f32[384]{0:T(512)S(1)}, u32[]{:S(2)}) copy-start(f32[384]{0:T(512)S(1)} %get-tuple-element.138) | copy-start | bytes 4612
  128.2 108.5 %copy-start.55 = (f32[384]{0:T(512)}, f32[384]{0:T(512)S(1)}, u32[]{:S(2)}) copy-start(f32[384]{0:T(512)S(1)} %get-tuple-element.139) | copy-start | bytes 4612
  128.2 108.5 %copy-start.56 = (f32[384]{0:T(512)}, f32[384]{0:T(512)S(1)}, u32[]{:S(2)}) copy-start(f32[384]{0:T(512)S(1)} %get-tuple-element.140) | copy-start | bytes 4612
  128.2 108.5 %copy-start.57 = (f32[384]{0:T(512)}, f32[384]{0:T(512)S(1)}, u32[]{:S(2)}) copy-start(f32[384]{0:T(512)S(1)} %get-tuple-element.141) | copy-start | bytes 4612
  128.2 108.5 %copy-start.58 = (f32[384]{0:T(512)}, f32[384]{0:T(512)S(1)}, u32[]{:S(2)}) copy-start(f32[384]{0:T(512)S(1)} %get-tuple-element.142) | copy-start | bytes 4612
  128.9 107.8 %copy-start.59 = (f32[384]{0:T(512)}, f32[384]{0:T(512)S(1)}, u32[]{:S(2)}) copy-start(f32[384]{0:T(512)S(1)} %get-tuple-element.125) | copy-start | bytes 4612
  128.9 107.8 %copy-start.60 = (f32[384]{0:T(512)}, f32[384]{0:T(512)S(1)}, u32[]{:S(2)}) copy-start(f32[384]{0:T(512)S(1)} %get-tuple-element.126) | copy-start | bytes 4612
  129.0 107.8 %copy-start.61 = (f32[384]{0:T(512)}, f32[384]{0:T(512)S(1)}, u32[]{:S(2)}) copy-start(f32[384]{0:T(512)S(1)} %get-tuple-element.127) | copy-start | bytes 4612
  129.0 107.9 %copy-start.62 = (f32[384]{0:T(512)}, f32[384]{0:T(512)S(1)}, u32[]{:S(2)}) copy-start(f32[384]{0:T(512)S(1)} %get-tuple-element.128) | copy-start | bytes 4612
  129.0 107.9 %copy-start.63 = (f32[384]{0:T(512)}, f32[384]{0:T(512)S(1)}, u32[]{:S(2)}) copy-start(f32[384]{0:T(512)S(1)} %get-tuple-element.129) | copy-start | bytes 4612
  129.0 107.9 %copy-start.64 = (f32[384]{0:T(512)}, f32[384]{0:T(512)S(1)}, u32[]{:S(2)}) copy-start(f32[384]{0:T(512)S(1)} %get-tuple-element.130) | copy-start | bytes 4612
  129.8 112.1 %copy-start.68 = (f32[384]{0:T(512)}, f32[384]{0:T(512)S(1)}, u32[]{:S(2)}) copy-start(f32[384]{0:T(512)S(1)} %get-tuple-element.229) | copy-start | bytes 4612
  132.2 111.3 %copy-start.20 = (bf16[384,1536]{1,0:T(8,128)(2,1)}, bf16[384,1536]{1,0:T(8,128)(2,1)S(1)}, u32[]{:S(2)}) copy-start(bf16[384,1536]{1,0:T(8,128)(2,1)S(1)} %constant_dynamic-update-slice_fusion) | copy-start | bytes 3538948
  273.5 32.4 %slice-start = ((s8[4325376]{0:T(1024)(128)(4,1)}), s8[131072]{0:T(1024)(128)(4,1)S(1)}, s32[]{:S(2)}) async-start(s8[4325376]{0:T(1024)(128)(4,1)} %bitcast.95), calls=%async_computation.3 | async-start | bytes 262144
  281.3 19.4 %copy-start.10 = (bf16[2816,384]{1,0:T(8,128)(2,1)S(1)}, bf16[2816,384]{1,0:T(8,128)(2,1)}, u32[]{:S(2)}) copy-start(bf16[2816,384]{1,0:T(8,128)(2,1)} %copy-done.9) | copy-start | bytes 6488068
  281.4 24.5 %slice-start.1 = ((s8[4325376]{0:T(1024)(128)(4,1)}), s8[4194304]{0:T(1024)(128)(4,1)S(1)}, s32[]{:S(2)}) async-start(s8[4325376]{0:T(1024)(128)(4,1)} %bitcast.95), calls=%async_computation.4 | async-start | bytes 8388608
  313.8 16.3 %slice-start.6 = ((s8[4325376]{0:T(1024)(128)(4,1)}), s8[131072]{0:T(1024)(128)(4,1)S(1)}, s32[]{:S(2)}) async-start(s8[4325376]{0:T(1024)(128)(4,1)} %bitcast.105), calls=%async_computation.9 | async-start | bytes 262144
  320.2 19.8 %slice-start.2 = ((s8[4325376]{0:T(1024)(128)(4,1)}), s8[4194304]{0:T(1024)(128)(4,1)S(1)}, s32[]{:S(2)}) async-start(s8[4325376]{0:T(1024)(128)(4,1)} %bitcast.97), calls=%async_computation.5 | async-start | bytes 8388608
  320.2 19.8 %slice-start.4 = ((s8[4325376]{0:T(1024)(128)(4,1)}), s8[4194304]{0:T(1024)(128)(4,1)S(1)}, s32[]{:S(2)}) async-start(s8[4325376]{0:T(1024)(128)(4,1)} %bitcast.103), calls=%async_computation.7 | async-start | bytes 8388608
  342.3 142.9 %copy-start.4 = (bf16[2816,384]{1,0:T(8,128)(2,1)}, bf16[2816,384]{1,0:T(8,128)(2,1)S(1)}, u32[]{:S(2)}) copy-start(bf16[2816,384]{1,0:T(8,128)(2,1)S(1)} %multiply_convert_fusion.1) | copy-start | bytes 6488068
  439.6 46.0 %collective-permute-start.10 = (f32[10944]{0:T(1024)S(1)}, f32[10944]{0:T(1024)S(1)}, u32[]{:S(2)}, u32[]{:S(2)}) collective-permute-start(f32[10944]{0:T(1024)S(1)} %pad_maximum_fusion.9), channel_id=1, source_target_pairs={{0,1},{1,0},{2,3},{3,2},{4,5},{5,4},{6,7},{7,6},{8,9},{9,8},{10,11... | collective-permute-start | bytes 131336 | tf_op jit(solution)/shard_map/ppermute | solution.py:13
  440.0 45.2 %collective-permute-start.7 = (bf16[3,176,384]{2,1,0:T(8,128)(2,1)}, bf16[3,176,384]{2,1,0:T(8,128)(2,1)S(1)}, u32[]{:S(2)}, u32[]{:S(2)}) collective-permute-start(bf16[3,176,384]{2,1,0:T(8,128)(2,1)} %bitcast.110), channel_id=1, source_target_pairs={{2,0},{4,2},{6,4},{8,6},{10,8},{12,10},{14,12},{16,14},{18,16},{20... | collective-permute-start | bytes 1216520 | tf_op jit(solution)/shard_map/ppermute | solution.py:21
  441.4 43.8 %collective-permute-start.6 = (bf16[3,176,384]{2,1,0:T(8,128)(2,1)S(1)}, bf16[3,176,384]{2,1,0:T(8,128)(2,1)S(1)}, u32[]{:S(2)}, u32[]{:S(2)}) collective-permute-start(bf16[3,176,384]{2,1,0:T(8,128)(2,1)S(1)} %bitcast.109), channel_id=1, source_target_pairs={{0,2},{2,4},{4,6},{6,8},{8,10},{10,12},{12,14},{14,16},{16,18},{18... | collective-permute-start | bytes 1216520 | tf_op jit(solution)/shard_map/ppermute | solution.py:20
  449.4 43.8 %collective-permute-start.11 = (f32[384,768]{1,0:T(8,128)}, f32[384,768]{1,0:T(8,128)}, u32[]{:S(2)}, u32[]{:S(2)}) collective-permute-start(f32[384,768]{1,0:T(8,128)} %slice.1161), channel_id=1, source_target_pairs={{0,1},{1,0},{2,3},{3,2},{4,5},{5,4},{6,7},{7,6},{8,9},{9,8},{10,11... | collective-permute-start | bytes 3538952 | tf_op jit(solution)/shard_map/ppermute | solution.py:13
  452.8 43.0 %collective-permute-start.12 = (f32[768,384]{0,1:T(8,128)}, f32[768,384]{0,1:T(8,128)}, u32[]{:S(2)}, u32[]{:S(2)}) collective-permute-start(f32[768,384]{0,1:T(8,128)} %slice.1166), channel_id=1, source_target_pairs={{0,1},{1,0},{2,3},{3,2},{4,5},{5,4},{6,7},{7,6},{8,9},{9,8},{10,11... | collective-permute-start | bytes 3538952 | tf_op jit(solution)/shard_map/ppermute | solution.py:13
  478.2 209.4 %all-to-all-start = ((bf16[32,16,3072]{2,1,0:T(8,128)(2,1)}), bf16[32,16,3072]{2,1,0:T(8,128)(2,1)}, u32[]{:S(2)}, u32[]{:S(2)}) async-start(bf16[32,16,3072]{2,1,0:T(8,128)(2,1)} %broadcast_select_fusion.2), calls=%async_computation | async-start | bytes 6291456 | tf_op jit(solution)/shard_map/all_to_all | solution.py:151
  485.1 196.2 %all-reduce.4.cloned.1.call-start = ((), (), s32[]{:S(2)}) async-start(), calls=%async_computation.2 | async-start | bytes 6119424
  485.3 1.4 collective-permute-start.8
  557.5 3.4 collective-permute-start.9
  (46 other events, 282.8 us)
Sparse Core Ops, SparseCore 0:
  498.4 182.9 all-reduce.3
